TPU v7x, 256 devices: a whole 4x4x8 slice. The times are simulated.
256 devices in a mesh: row: 32 (over y, z), col: 8 (over x, core).
Axes of the slice: x: 4, y: 4, z: 8, core: 2. Of those that a mesh axis runs over, the one named last changes fastest.
Arguments:
- queries: bfloat16 [16384, 1024], P(('row', 'col'))
- passages: bfloat16 [32768, 1024], P(('col', 'row'))
- positives: int32 [16384], P('row'), may hold values from 0 to 32767
Outputs:
- losses: float32 [16384], P('row')
- query_grad: float32 [16384, 1024], P(('row', 'col'))
- passage_grad: float32 [32768, 1024], P(('col', 'row'))
All inputs are finite; a program needn't handle non-finite values.
Results may differ from a plain program's by a relative error of at most 0.0022.
Values may be sent and summed in bfloat16 or wider, within the bound.
No kernel may reach another device: no remote copies, remote signals or barrier semaphores. Data moves between devices by JAX's collectives and lax.ppermute only.
A program may use at most 128 MiB of HBM per device.

v0:
```python
import math
import jax
import jax.numpy as jnp
from jax import lax
from jax.sharding import PartitionSpec as P

D = 1024


def body(queries, passages, positives):
    scale = 3.0 / math.sqrt(D)
    query_full = lax.all_gather(queries, "col", axis=0, tiled=True)
    passage_full = lax.all_gather(passages, "row", axis=0, tiled=True)
    scores = (
        lax.dot_general(
            query_full, passage_full, (((1,), (1,)), ((), ())), preferred_element_type=jnp.float32
        )
        * scale
    )
    passage_count = passage_full.shape[0]
    first_column = lax.axis_index("col") * passage_count
    column = lax.broadcasted_iota(jnp.int32, scores.shape, 1) + first_column
    hit = column == positives[:, None]
    local_score = jnp.sum(jnp.where(hit, scores, 0.0), axis=1)
    top = lax.pmax(jnp.max(scores, axis=1), "col")
    total, pos_score = lax.psum(
        (jnp.sum(jnp.exp(scores - top[:, None]), axis=1), local_score), "col"
    )
    lse = top + jnp.log(total)
    losses = lse - pos_score
    weights = ((jnp.exp(scores - lse[:, None]) - hit.astype(jnp.float32)) * scale).astype(
        jnp.bfloat16
    )
    query_grad = lax.psum_scatter(
        jnp.dot(weights, passage_full, preferred_element_type=jnp.float32),
        "col",
        scatter_dimension=0,
        tiled=True,
    )
    passage_grad = lax.psum_scatter(
        lax.dot_general(
            weights, query_full, (((0,), (0,)), ((), ())), preferred_element_type=jnp.float32
        ),
        "row",
        scatter_dimension=0,
        tiled=True,
    )
    return (losses, query_grad, passage_grad)


def solution(mesh):
    return jax.shard_map(
        body,
        mesh=mesh,
        in_specs=(P(("row", "col"), None), P(("col", "row"), None), P("row")),
        out_specs=(P("row"), P(("row", "col"), None), P(("col", "row"), None)),
        check_vma=False,
    )
```

profile of v0, /device:TPU:2, one launch (start us, length us, event | category | flops | bytes accessed | tf_op | source)
XLA Modules:
  0.0 483.9 jit_solution(17748731228473105264)
XLA Ops:
  7.2 0.0 all-gather.3.cloned.1.call-start
  7.2 0.7 all-gather.3.cloned.1.call-update
  7.9 0.0 all-gather.5.cloned.1.call-start
  7.9 0.7 all-gather.5.cloned.1.call-update
  8.6 0.0 reduce-scatter.3.cloned.1.call-start
  8.7 0.0 copy-start.1
  8.7 28.4 %all-gather.3.cloned.1.call-done = bf16[512,1024]{1,0:T(8,128)(2,1)} async-done(((bf16[64,1024]{1,0:T(8,128)(2,1)}), bf16[512,1024]{1,0:T(8,128)(2,1)}) %all-gather.3.cloned.1.call-update) | async-done | bytes 1048592 | tf_op jit(solution)/shard_map/all_gather | solution.py:12
  37.1 102.7 %all-gather.5.cloned.1.call-done = bf16[4096,1024]{1,0:T(8,128)(2,1)} async-done(((bf16[128,1024]{1,0:T(8,128)(2,1)}), bf16[4096,1024]{1,0:T(8,128)(2,1)}) %all-gather.5.cloned.1.call-update) | async-done | bytes 8388624 | tf_op jit(solution)/shard_map/all_gather | solution.py:13
  139.8 11.5 %multiply_reduce_fusion = (f32[512]{0:T(512)S(1)}, f32[512,4096]{1,0:T(8,128)}) fusion(bf16[512,1024]{1,0:T(8,128)(2,1)} %all-gather.3.cloned.1.call-done, bf16[4096,1024]{1,0:T(8,128)(2,1)} %all-gather.5.cloned.1.call-done), kind=kOutput, calls=%fused_computation.7 | convolution fusion | flops 4299161088 | bytes 17827840 | tf_op jit(solution)/shard_map/dot_general | solution.py:15
  151.3 11.2 %pmax.7 = f32[512]{0:T(512)S(1)} all-reduce(f32[512]{0:T(512)S(1)} %get-tuple-element.9), channel_id=1, replica_groups=mesh['row'=32,'col'=8] {'col'}, use_global_device_ids=true, to_apply=%region_1.2 | all-reduce | flops 512 | bytes 4096 | tf_op jit(solution)/shard_map/pmax | solution.py:25
  162.4 0.0 copy-done.1
  162.5 5.0 %fusion = (f32[512]{0:T(512)S(1)}, f32[512]{0:T(512)S(1)}) fusion(f32[512,4096]{1,0:T(8,128)} %get-tuple-element.10, s32[4096]{0:T(1024)S(1)} %iota_add_fusion, s32[512]{0:T(512)S(1)} %copy-done.1, f32[512]{0:T(512)S(1)} %pmax.7), kind=kLoop, calls=%fused_computation.2 | loop fusion | flops 12581888 | bytes 8413184 | tf_op jit(solution)/shard_map/reduce_sum | solution.py:24
  167.5 12.4 %all-reduce = (f32[512]{0:T(512)S(1)}, f32[512]{0:T(512)S(1)}) all-reduce(f32[512]{0:T(512)S(1)} %get-tuple-element.4, f32[512]{0:T(512)S(1)} %get-tuple-element.3), channel_id=1, replica_groups=mesh['row'=32,'col'=8] {'col'}, use_global_device_ids=true, to_apply=%region_3.4 | all-reduce | flops 1024 | bytes 8192 | tf_op jit(solution)/shard_map/psum | solution.py:26
  179.9 0.6 fusion.4
  180.5 4.8 fusion.3
  185.4 0.0 copy-start
  185.4 1.9 copy-done
  187.3 0.0 copy-start.2
  187.3 8.3 %fusion.5 = f32[512,1024]{1,0:T(8,128)} fusion(bf16[512,4096]{1,0:T(8,128)(2,1)S(1)} %fusion.3, bf16[4096,1024]{1,0:T(8,128)(2,1)} %all-gather.5.cloned.1.call-done), kind=kOutput, calls=%fused_computation.11 | convolution fusion | flops 4294967296 | bytes 14680064 | tf_op jit(solution)/shard_map/dot_general | solution.py:35
  195.6 0.0 reduce-scatter.3.cloned.1.call-update
  195.6 0.0 reduce-scatter.5.cloned.1.call-start
  195.6 0.0 copy-done.2
  195.7 10.6 %fusion.6 = f32[4096,1024]{1,0:T(8,128)} fusion(bf16[512,4096]{1,0:T(8,128)(2,1)} %copy-done, bf16[512,1024]{1,0:T(8,128)(2,1)S(1)} %copy-done.2), kind=kOutput, calls=%fused_computation.12 | convolution fusion | flops 4294967296 | bytes 22020096 | tf_op jit(solution)/shard_map/dot_general | solution.py:41
  206.2 0.0 reduce-scatter.5.cloned.1.call-update
  206.3 20.0 %reduce-scatter.3.cloned.1.call-done = f32[64,1024]{1,0:T(8,128)} async-done(((f32[512,1024]{1,0:T(8,128)}), f32[64,1024]{1,0:T(8,128)}) %reduce-scatter.3.cloned.1.call-update) | async-done | bytes 262160 | tf_op jit(solution)/shard_map/reduce_scatter | solution.py:34
  226.2 251.1 %reduce-scatter.5.cloned.1.call-done = f32[128,1024]{1,0:T(8,128)} async-done(((f32[4096,1024]{1,0:T(8,128)}), f32[128,1024]{1,0:T(8,128)}) %reduce-scatter.5.cloned.1.call-update) | async-done | bytes 524304 | tf_op jit(solution)/shard_map/reduce_scatter | solution.py:40
  (1 shorter events, 0.0 us)
Async XLA Ops:
  7.2 29.9 %all-gather.3.cloned.1.call-start = ((), (), s32[]{:S(2)}) async-start(), calls=%async_computation.2 | async-start | bytes 1179648 | tf_op jit(solution)/shard_map/all_gather | solution.py:12
  7.9 131.9 %all-gather.5.cloned.1.call-start = ((), (), s32[]{:S(2)}) async-start(), calls=%async_computation.3 | async-start | bytes 8650752 | tf_op jit(solution)/shard_map/all_gather | solution.py:13
  8.6 217.6 %reduce-scatter.3.cloned.1.call-start = ((), (), s32[]{:S(2)}) async-start(), calls=%async_computation.4 | async-start | bytes 2359296 | tf_op jit(solution)/shard_map/reduce_scatter | solution.py:34
  8.7 153.7 %copy-start.1 = (s32[512]{0:T(512)S(1)}, s32[512]{0:T(512)}, u32[]{:S(2)}) copy-start(s32[512]{0:T(512)} %param.5) | copy-start | bytes 6148
  185.4 1.9 copy-start
  187.3 8.4 %copy-start.2 = (bf16[512,1024]{1,0:T(8,128)(2,1)S(1)}, bf16[512,1024]{1,0:T(8,128)(2,1)}, u32[]{:S(2)}) copy-start(bf16[512,1024]{1,0:T(8,128)(2,1)} %all-gather.3.cloned.1.call-done) | copy-start | bytes 3145732
  195.6 281.7 %reduce-scatter.5.cloned.1.call-start = ((), (), s32[]{:S(2)}) async-start(), calls=%async_computation.5 | async-start | bytes 17301504 | tf_op jit(solution)/shard_map/reduce_scatter | solution.py:40
Sparse Core Ops, SparseCore 0:
  9.9 27.1 all-gather.2
  39.7 100.0 all-gather.4
  195.7 30.4 reduce-scatter.2
  230.8 246.5 reduce-scatter.4
where the time goes:
time: 484 us
  waiting for transfers between devices  404 us (83%)
  matrix products  30.3 us (6%)
  blocking collectives  23.6 us (5%)
  between operations  13.8 us (3%)
  other arithmetic  10.5 us (2%)
    reduce_scatter x1, waiting for transfers between devices, body(): lax.psum_scatter(lax.dot_general(weights, query_full, (((0,), (0,)), ((),...  251 us
    all_gather x1, waiting for transfers between devices, body(): passage_full = lax.all_gather(passages, 'row', axis=0, tiled=True)  103 us
    all_gather x1, waiting for transfers between devices, body(): query_full = lax.all_gather(queries, 'col', axis=0, tiled=True)  28.4 us
    reduce_scatter x1, waiting for transfers between devices, body(): lax.psum_scatter(jnp.dot(weights, passage_full, preferred_element_type=jn...  20 us
    psum x1, blocking collectives, body(): lax.psum((jnp.sum(jnp.exp(scores - top[:, None]), axis=1), local_score),...  12.4 us
    dot_general x1, matrix products, body(): lax.dot_general(query_full, passage_full, (((1,), (1,)), ((), ())), prefe...  11.5 us
    pmax x1, blocking collectives, body(): top = lax.pmax(jnp.max(scores, axis=1), 'col')  11.2 us
    dot_general x1, matrix products, body(): lax.dot_general(weights, query_full, (((0,), (0,)), ((), ())), preferred_...  10.6 us
  transfers between devices with their start and end apart: 4, of which 4 were waited for; matrix products, arithmetic and copies ran while one was open for 2% of the time, Pallas kernels for 0%

commit v1 on v0

--- a/solution.py
+++ b/solution.py
@@ -9,7 +9,9 @@
 
 def body(queries, passages, positives):
     scale = 3.0 / math.sqrt(D)
-    query_full = lax.all_gather(queries, "col", axis=0, tiled=True)
+    query_full = jnp.concatenate(
+        lax.all_to_all(jnp.stack([queries] * lax.axis_size("col")), "col", 0, 0), axis=0
+    )
     passage_full = lax.all_gather(passages, "row", axis=0, tiled=True)
     scores = (
         lax.dot_general(

time: 484 us -> 455 us (0.940)
  waiting for transfers between devices: 404 us -> 369 us
  starting transfers between devices: 0.16 us -> 5.82 us
    all_gather x1 -> x0, waiting for transfers between devices: 28.4 us -> none  [body(): query_full = lax.all_gather(queries, 'col', axis=0, tiled=True)]
    all_gather x1, waiting for transfers between devices: 103 us -> 81.8 us  [body(): passage_full = lax.all_gather(passages, 'row', axis=0, tiled=True)]
    all_to_all x0 -> x1, waiting for transfers between devices: none -> 14.5 us  [body(): lax.all_to_all(jnp.stack([queries] * lax.axis_size('col')), 'col', 0, 0)]
    all_to_all x0 -> x1, starting transfers between devices: none -> 5.74 us  [body(): lax.all_to_all(jnp.stack([queries] * lax.axis_size('col')), 'col', 0, 0)]
  transfers between devices with their start and end apart: 4 -> 4, of which waited for: 4 -> 4; matrix products, arithmetic and copies ran while one was open for 2% -> 3% of each run, Pallas kernels for 0% -> 0%
where the time goes in v1:
time: 455 us
  waiting for transfers between devices  369 us (81%)
  matrix products  29 us (6%)
  blocking collectives  23.6 us (5%)
  between operations  13.8 us (3%)
  other arithmetic  10.5 us (2%)
  starting transfers between devices  5.82 us (1%)
    reduce_scatter x1, waiting for transfers between devices, body(): lax.psum_scatter(lax.dot_general(weights, query_full, (((0,), (0,)), ((),...  251 us
    all_gather x1, waiting for transfers between devices, body(): passage_full = lax.all_gather(passages, 'row', axis=0, tiled=True)  81.8 us
    reduce_scatter x1, waiting for transfers between devices, body(): lax.psum_scatter(jnp.dot(weights, passage_full, preferred_element_type=jn...  20 us
    all_to_all x1, waiting for transfers between devices, body(): lax.all_to_all(jnp.stack([queries] * lax.axis_size('col')), 'col', 0, 0)  14.5 us
    psum x1, blocking collectives, body(): lax.psum((jnp.sum(jnp.exp(scores - top[:, None]), axis=1), local_score),...  12.4 us
    pmax x1, blocking collectives, body(): top = lax.pmax(jnp.max(scores, axis=1), 'col')  11.2 us
    dot_general x1, matrix products, body(): lax.dot_general(weights, query_full, (((0,), (0,)), ((), ())), preferred_...  10.6 us
    dot_general x1, matrix products, body(): lax.dot_general(query_full, passage_full, (((1,), (1,)), ((), ())), prefe...  10.2 us
  transfers between devices with their start and end apart: 4, of which 4 were waited for; matrix products, arithmetic and copies ran while one was open for 3% of the time, Pallas kernels for 0%

profile of v1, /device:TPU:2, one launch (start us, length us, event | category | flops | bytes accessed | tf_op | source)
XLA Modules:
  0.0 455.2 jit_solution(17937576922104830614)
XLA Ops:
  7.2 0.0 all-gather.2.cloned.1.call-start
  7.2 0.7 all-gather.2.cloned.1.call-update
  7.9 2.1 stack.2
  10.0 5.7 %all-to-all-start = ((bf16[8,64,1024]{2,1,0:T(8,128)(2,1)}), bf16[8,64,1024]{2,1,0:T(8,128)(2,1)S(1)}, u32[]{:S(2)}, u32[]{:S(2)}) async-start(bf16[8,64,1024]{2,1,0:T(8,128)(2,1)} %stack.2), calls=%async_computation | async-start | bytes 2097152 | tf_op jit(solution)/shard_map/all_to_all | solution.py:13
  15.7 0.0 reduce-scatter.3.cloned.1.call-start
  15.7 14.5 %all-to-all-done = bf16[8,64,1024]{2,1,0:T(8,128)(2,1)S(1)} async-done(((bf16[8,64,1024]{2,1,0:T(8,128)(2,1)}), bf16[8,64,1024]{2,1,0:T(8,128)(2,1)S(1)}, u32[]{:S(2)}, u32[]{:S(2)}) %all-to-all-start) | async-done | bytes 1048608 | tf_op jit(solution)/shard_map/all_to_all | solution.py:13
  30.3 81.8 %all-gather.2.cloned.1.call-done = bf16[4096,1024]{1,0:T(8,128)(2,1)} async-done(((bf16[128,1024]{1,0:T(8,128)(2,1)}), bf16[4096,1024]{1,0:T(8,128)(2,1)}) %all-gather.2.cloned.1.call-update) | async-done | bytes 8388624 | tf_op jit(solution)/shard_map/all_gather | solution.py:15
  112.1 0.0 copy-start.1
  112.1 10.2 %multiply_reduce_fusion = (f32[512]{0:T(512)S(1)}, f32[512,4096]{1,0:T(8,128)}) fusion(bf16[512,1024]{1,0:T(8,128)(2,1)S(1)} %bitcast.7, bf16[4096,1024]{1,0:T(8,128)(2,1)} %all-gather.2.cloned.1.call-done), kind=kOutput, calls=%fused_computation.7 | convolution fusion | flops 4299161088 | bytes 17827840 | tf_op jit(solution)/shard_map/dot_general | solution.py:17
  122.3 11.2 %pmax.7 = f32[512]{0:T(512)S(1)} all-reduce(f32[512]{0:T(512)S(1)} %get-tuple-element.9), channel_id=1, replica_groups=mesh['row'=32,'col'=8] {'col'}, use_global_device_ids=true, to_apply=%region_1.2 | all-reduce | flops 512 | bytes 4096 | tf_op jit(solution)/shard_map/pmax | solution.py:27
  133.5 0.0 copy-done.1
  133.5 5.0 %fusion = (f32[512]{0:T(512)S(1)}, f32[512]{0:T(512)S(1)}) fusion(f32[512,4096]{1,0:T(8,128)} %get-tuple-element.10, s32[4096]{0:T(1024)S(1)} %iota_add_fusion, s32[512]{0:T(512)S(1)} %copy-done.1, f32[512]{0:T(512)S(1)} %pmax.7), kind=kLoop, calls=%fused_computation.2 | loop fusion | flops 12581888 | bytes 8413184 | tf_op jit(solution)/shard_map/reduce_sum | solution.py:26
  138.5 12.4 %all-reduce = (f32[512]{0:T(512)S(1)}, f32[512]{0:T(512)S(1)}) all-reduce(f32[512]{0:T(512)S(1)} %get-tuple-element.4, f32[512]{0:T(512)S(1)} %get-tuple-element.3), channel_id=1, replica_groups=mesh['row'=32,'col'=8] {'col'}, use_global_device_ids=true, to_apply=%region_3.4 | all-reduce | flops 1024 | bytes 8192 | tf_op jit(solution)/shard_map/psum | solution.py:28
  150.9 0.6 fusion.4
  151.5 4.8 %fusion.3 = bf16[512,4096]{1,0:T(8,128)(2,1)S(1)} fusion(f32[512,4096]{1,0:T(8,128)} %get-tuple-element.10, f32[512]{0:T(512)S(1)} %get-tuple-element.8, s32[4096]{0:T(1024)S(1)} %iota_add_fusion, s32[512]{0:T(512)S(1)} %copy-done.1), kind=kLoop, calls=%fused_computation.5 | loop fusion | flops 14680064 | bytes 12603392 | tf_op jit(solution)/shard_map/convert_element_type | solution.py:33
  156.4 0.0 copy-start
  156.4 1.9 copy-done
  158.3 8.2 %fusion.5 = f32[512,1024]{1,0:T(8,128)} fusion(bf16[512,4096]{1,0:T(8,128)(2,1)S(1)} %fusion.3, bf16[4096,1024]{1,0:T(8,128)(2,1)} %all-gather.2.cloned.1.call-done), kind=kOutput, calls=%fused_computation.11 | convolution fusion | flops 4294967296 | bytes 14680064 | tf_op jit(solution)/shard_map/dot_general | solution.py:37
  166.5 0.0 reduce-scatter.3.cloned.1.call-update
  166.5 0.0 reduce-scatter.5.cloned.1.call-start
  166.6 10.6 %fusion.6 = f32[4096,1024]{1,0:T(8,128)} fusion(bf16[512,4096]{1,0:T(8,128)(2,1)} %copy-done, bf16[512,1024]{1,0:T(8,128)(2,1)S(1)} %bitcast.8), kind=kOutput, calls=%fused_computation.12 | convolution fusion | flops 4294967296 | bytes 22020096 | tf_op jit(solution)/shard_map/dot_general | solution.py:43
  177.2 0.0 reduce-scatter.5.cloned.1.call-update
  177.2 20.0 %reduce-scatter.3.cloned.1.call-done = f32[64,1024]{1,0:T(8,128)} async-done(((f32[512,1024]{1,0:T(8,128)}), f32[64,1024]{1,0:T(8,128)}) %reduce-scatter.3.cloned.1.call-update) | async-done | bytes 262160 | tf_op jit(solution)/shard_map/reduce_scatter | solution.py:36
  197.2 251.5 %reduce-scatter.5.cloned.1.call-done = f32[128,1024]{1,0:T(8,128)} async-done(((f32[4096,1024]{1,0:T(8,128)}), f32[128,1024]{1,0:T(8,128)}) %reduce-scatter.5.cloned.1.call-update) | async-done | bytes 524304 | tf_op jit(solution)/shard_map/reduce_scatter | solution.py:42
  (1 shorter events, 0.0 us)
Async XLA Ops:
  7.2 104.9 %all-gather.2.cloned.1.call-start = ((), (), s32[]{:S(2)}) async-start(), calls=%async_computation.3 | async-start | bytes 8650752 | tf_op jit(solution)/shard_map/all_gather | solution.py:15
  10.0 20.3 %all-to-all-start = ((bf16[8,64,1024]{2,1,0:T(8,128)(2,1)}), bf16[8,64,1024]{2,1,0:T(8,128)(2,1)S(1)}, u32[]{:S(2)}, u32[]{:S(2)}) async-start(bf16[8,64,1024]{2,1,0:T(8,128)(2,1)} %stack.2), calls=%async_computation | async-start | bytes 2097152 | tf_op jit(solution)/shard_map/all_to_all | solution.py:13
  15.7 181.5 %reduce-scatter.3.cloned.1.call-start = ((), (), s32[]{:S(2)}) async-start(), calls=%async_computation.4 | async-start | bytes 2359296 | tf_op jit(solution)/shard_map/reduce_scatter | solution.py:36
  112.1 21.4 %copy-start.1 = (s32[512]{0:T(512)S(1)}, s32[512]{0:T(512)}, u32[]{:S(2)}) copy-start(s32[512]{0:T(512)} %param.5) | copy-start | bytes 6148
  156.4 1.9 copy-start
  166.5 282.1 %reduce-scatter.5.cloned.1.call-start = ((), (), s32[]{:S(2)}) async-start(), calls=%async_computation.5 | async-start | bytes 17301504 | tf_op jit(solution)/shard_map/reduce_scatter | solution.py:42
Sparse Core Ops, SparseCore 0:
  10.6 101.4 all-gather.1
  166.6 30.4 reduce-scatter.2
  201.9 246.7 reduce-scatter.4
